TPU v7x, 128 devices: a whole 4x4x4 slice. The times are simulated.
128 devices in a mesh: ctx: 32 (over y, z, x_lo), wa: 4 (over x_hi, core).
Axes of the slice: x: 4 (x_hi: 2, x_lo: 2; x = x_hi * 2 + x_lo), y: 4, z: 4, core: 2. Of those that a mesh axis runs over, the one named last changes fastest.
Arguments:
- inputs: bfloat16 [4, 6144, 1024], P('wa', 'ctx'), may hold values from -6 to 6
- first_gain: bfloat16 [1024], P('wa'), may hold values from 0.5 to 1.5
- first_bias: bfloat16 [1024], P('wa'), may hold values from -1.796875 to 1.796875
- second_gain: bfloat16 [1024], P('wa'), may hold values from 0.5 to 1.5
- second_bias: bfloat16 [1024], P('wa'), may hold values from -1.796875 to 1.796875
- mix_weight: bfloat16 [1024, 3072], P('wa'), may hold values from -0.1875 to 0.1875
- mix_bias: bfloat16 [3072], P('wa'), may hold values from -1.796875 to 1.796875
- dense_weight: bfloat16 [1024, 1024], P('wa'), may hold values from -1.5 to 1.5
- dense_bias: bfloat16 [1024], P('wa'), may hold values from -1.796875 to 1.796875
- up_weight: bfloat16 [1024, 4096], P('wa'), may hold values from -0.1875 to 0.1875
- up_bias: bfloat16 [4096], P('wa'), may hold values from -1.796875 to 1.796875
- down_weight: bfloat16 [4096, 1024], P('wa'), may hold values from -0.09375 to 0.09375
- down_bias: bfloat16 [1024], P('wa'), may hold values from -1.796875 to 1.796875
- grad_out: bfloat16 [4, 6144, 1024], P('wa', 'ctx'), may hold values from -6 to 6
Outputs:
- output: bfloat16 [4, 6144, 1024], P('wa', 'ctx')
- grad_inputs: bfloat16 [4, 6144, 1024], P('wa', 'ctx')
- grad_first_gain: float32 [1024], P('wa')
- grad_first_bias: float32 [1024], P('wa')
- grad_second_gain: float32 [1024], P('wa')
- grad_second_bias: float32 [1024], P('wa')
- grad_mix_weight: float32 [1024, 3072], P('wa')
- grad_mix_bias: float32 [3072], P('wa')
- grad_dense_weight: float32 [1024, 1024], P('wa')
- grad_dense_bias: float32 [1024], P('wa')
- grad_up_weight: float32 [1024, 4096], P('wa')
- grad_up_bias: float32 [4096], P('wa')
- grad_down_weight: float32 [4096, 1024], P('wa')
- grad_down_bias: float32 [1024], P('wa')
All inputs are finite; a program needn't handle non-finite values.
Results may differ from a plain program's by a relative error of at most 0.025.
Values may be sent and summed in bfloat16 or wider, within the bound.
No kernel may reach another device: no remote copies, remote signals or barrier semaphores. Data moves between devices by JAX's collectives and lax.ppermute only.
A program may use at most 384 MiB of HBM per device.

v0:
```python
import jax
import jax.numpy as jnp
from jax import lax
from jax.sharding import PartitionSpec as P

D = 1024
HEADS = 16
HDIM = 64
ROT = 16


epsilon = 1e-05
masked = -1e30


def layer_norm(values, scale_vec, shift_vec):
    centre = jnp.mean(values, -1, keepdims=True)
    centred = values - centre
    spread = jnp.mean(centred * centred, -1, keepdims=True)
    return centred * lax.rsqrt(spread + epsilon) * scale_vec + shift_vec


def rotary_tables(positions):
    exponents = jnp.arange(0, ROT, 2, dtype=jnp.float32) / ROT
    inverse = 1.0 / 10000.0**exponents
    angles = positions[:, None] * inverse[None, :]
    doubled = jnp.concatenate([angles, angles], -1)
    return (jnp.cos(doubled), jnp.sin(doubled))


def rotate(values, cos_table, sin_table):
    rot_width = cos_table.shape[-1]
    half_width = rot_width // 2
    rotary_part = values[..., :rot_width]
    first_half = rotary_part[..., :half_width]
    second_half = rotary_part[..., half_width:]
    turned = jnp.concatenate([-second_half, first_half], -1)
    return jnp.concatenate(
        [rotary_part * cos_table + turned * sin_table, values[..., rot_width:]], -1
    )


def gelu_exact(values):
    return jax.nn.gelu(values, approximate=False)


def attention_probs(queries, query_pos, key_heads, key_pos, log_total):
    scores = jnp.einsum(
        "qhd,khd->hqk", queries, key_heads, preferred_element_type=jnp.float32
    ) * HDIM ** (-0.5)
    allowed = key_pos[None, :] <= query_pos[:, None]
    scores = jnp.where(allowed[None], scores, masked)
    return jnp.exp(scores - log_total[:, :, None])


def score_grads(prob_table, grad_heads, value_heads, delta_cols):
    d_probs = jnp.einsum(
        "qhd,khd->hqk", grad_heads, value_heads, preferred_element_type=jnp.float32
    )
    return (prob_table * (d_probs - delta_cols[:, :, None])).astype(jnp.bfloat16)


def shards(
    inputs,
    first_gain,
    first_bias,
    second_gain,
    second_bias,
    mix_weight,
    mix_bias,
    dense_weight,
    dense_bias,
    up_weight,
    up_bias,
    down_weight,
    down_bias,
    grad_out,
):
    row_count = inputs.shape[1]
    score_scale = HDIM ** (-0.5)
    gathered = (
        lax.all_gather(first_gain, "wa", axis=0, tiled=True),
        lax.all_gather(first_bias, "wa", axis=0, tiled=True),
        lax.all_gather(second_gain, "wa", axis=0, tiled=True),
        lax.all_gather(second_bias, "wa", axis=0, tiled=True),
        lax.all_gather(mix_weight, "wa", axis=0, tiled=True),
        lax.all_gather(mix_bias, "wa", axis=0, tiled=True),
        lax.all_gather(dense_weight, "wa", axis=0, tiled=True),
        lax.all_gather(dense_bias, "wa", axis=0, tiled=True),
        lax.all_gather(up_weight, "wa", axis=0, tiled=True),
        lax.all_gather(up_bias, "wa", axis=0, tiled=True),
        lax.all_gather(down_weight, "wa", axis=0, tiled=True),
        lax.all_gather(down_bias, "wa", axis=0, tiled=True),
    )
    flat_in = inputs[0].astype(jnp.float32)
    gain_one = gathered[0].astype(jnp.float32)
    shift_one = gathered[1].astype(jnp.float32)
    gain_two = gathered[2].astype(jnp.float32)
    shift_two = gathered[3].astype(jnp.float32)
    norm_one = layer_norm(flat_in, gain_one, shift_one).astype(jnp.bfloat16)
    norm_two = layer_norm(flat_in, gain_two, shift_two).astype(jnp.bfloat16)
    mixed_rows = jnp.dot(norm_one, gathered[4], preferred_element_type=jnp.float32) + gathered[
        5
    ].astype(jnp.float32)
    mixed_rows = mixed_rows.reshape(row_count, 3, HEADS, HDIM)
    own_first = lax.axis_index("ctx") * row_count
    query_pos = own_first + jnp.arange(row_count, dtype=jnp.int32)
    cos_table, sin_table = rotary_tables(query_pos.astype(jnp.float32))
    cos_full = cos_table[:, None, None, :]
    sin_full = sin_table[:, None, None, :]

    def turn_pair(values):
        return rotate(values, cos_full, sin_full)

    pair_raw = mixed_rows[:, 0:2]
    pair_low = turn_pair(pair_raw).astype(jnp.bfloat16)
    query_low = pair_low[:, 0]
    key_low = pair_low[:, 1]
    value_low = mixed_rows[:, 2].astype(jnp.bfloat16)
    run_max = jnp.full((HEADS, row_count), masked, jnp.float32)
    key_piece = lax.all_gather(key_low.reshape(row_count, D), "ctx", axis=0, tiled=True)
    value_piece = lax.all_gather(value_low.reshape(row_count, D), "ctx", axis=0, tiled=True)
    piece_rows = key_piece.shape[0]
    key_heads = key_piece.reshape(piece_rows, HEADS, HDIM)
    value_heads = value_piece.reshape(piece_rows, HEADS, HDIM)
    key_pos = jnp.arange(piece_rows, dtype=jnp.int32)
    scores = (
        jnp.einsum("qhd,khd->hqk", query_low, key_heads, preferred_element_type=jnp.float32)
        * score_scale
    )
    allowed = key_pos[None, :] <= query_pos[:, None]
    scores = jnp.where(allowed[None], scores, masked)
    new_max = jnp.maximum(run_max, jnp.max(scores, -1))
    weights = jnp.where(allowed[None], jnp.exp(scores - new_max[:, :, None]), 0.0)
    run_total = jnp.sum(weights, -1)
    weighted = jnp.einsum(
        "hqk,khd->hqd",
        weights.astype(jnp.bfloat16),
        value_heads,
        preferred_element_type=jnp.float32,
    )
    run_max, run_total, weighted = (new_max, run_total, weighted)
    heads_out = weighted / run_total[:, :, None]
    log_total = run_max + jnp.log(run_total)
    merged = heads_out.transpose(1, 0, 2).reshape(row_count, D)
    merged_low = merged.astype(jnp.bfloat16)
    attention = jnp.dot(merged_low, gathered[6], preferred_element_type=jnp.float32) + gathered[
        7
    ].astype(jnp.float32)
    up_pre = jnp.dot(norm_two, gathered[8], preferred_element_type=jnp.float32) + gathered[
        9
    ].astype(jnp.float32)
    hidden_low = gelu_exact(up_pre).astype(jnp.bfloat16)
    feed_out = jnp.dot(hidden_low, gathered[10], preferred_element_type=jnp.float32) + gathered[
        11
    ].astype(jnp.float32)
    output = (flat_in + attention + feed_out).astype(jnp.bfloat16)[None]
    gathered = (
        lax.all_gather(first_gain, "wa", axis=0, tiled=True),
        lax.all_gather(first_bias, "wa", axis=0, tiled=True),
        lax.all_gather(second_gain, "wa", axis=0, tiled=True),
        lax.all_gather(second_bias, "wa", axis=0, tiled=True),
        lax.all_gather(mix_weight, "wa", axis=0, tiled=True),
        lax.all_gather(mix_bias, "wa", axis=0, tiled=True),
        lax.all_gather(dense_weight, "wa", axis=0, tiled=True),
        lax.all_gather(dense_bias, "wa", axis=0, tiled=True),
        lax.all_gather(up_weight, "wa", axis=0, tiled=True),
        lax.all_gather(up_bias, "wa", axis=0, tiled=True),
        lax.all_gather(down_weight, "wa", axis=0, tiled=True),
        lax.all_gather(down_bias, "wa", axis=0, tiled=True),
    )
    upstream = grad_out[0]
    grad_bias_out = jnp.sum(upstream.astype(jnp.float32), 0)
    d_merged = jnp.einsum(
        "te,de->td", upstream, gathered[6], preferred_element_type=jnp.float32
    ).astype(jnp.bfloat16)
    d_hidden = jnp.einsum("td,fd->tf", upstream, gathered[10], preferred_element_type=jnp.float32)
    gelu_back = jax.vjp(gelu_exact, up_pre)[1]
    d_pre = gelu_back(d_hidden)[0].astype(jnp.bfloat16)
    grad_up_bias = jnp.sum(d_pre.astype(jnp.float32), 0)
    d_norm_two = jnp.einsum("tf,df->td", d_pre, gathered[8], preferred_element_type=jnp.float32)
    grad_heads = d_merged.reshape(row_count, HEADS, HDIM)
    delta_rows = jnp.sum(
        (d_merged.astype(jnp.float32) * merged).reshape(row_count, HEADS, HDIM), -1
    )
    delta_cols = delta_rows.T
    pieces = (
        lax.all_gather(key_low.reshape(row_count, D), "ctx", axis=0, tiled=True),
        lax.all_gather(value_low.reshape(row_count, D), "ctx", axis=0, tiled=True),
    )
    key_piece, value_piece = pieces
    piece_rows = key_piece.shape[0]
    key_heads = key_piece.reshape(piece_rows, HEADS, HDIM)
    value_heads = value_piece.reshape(piece_rows, HEADS, HDIM)
    key_pos = jnp.arange(piece_rows, dtype=jnp.int32)
    prob_table = attention_probs(query_low, query_pos, key_heads, key_pos, log_total)
    d_scores = score_grads(prob_table, grad_heads, value_heads, delta_cols)
    d_query = (
        jnp.einsum("hqk,khd->qhd", d_scores, key_heads, preferred_element_type=jnp.float32)
        * score_scale
    )
    prob_table, d_scores, d_query = (prob_table, d_scores, d_query)
    piece_rows = pieces[0].shape[0]
    d_key = (
        jnp.einsum("hqk,qhd->khd", d_scores, query_low, preferred_element_type=jnp.float32)
        * score_scale
    )
    d_value = jnp.einsum(
        "hqk,qhd->khd",
        prob_table.astype(jnp.bfloat16),
        grad_heads,
        preferred_element_type=jnp.float32,
    )
    key_terms = jnp.concatenate([d_key.reshape(piece_rows, D), d_value.reshape(piece_rows, D)], 1)
    back_state = (d_query, key_terms)
    d_query = back_state[0]
    key_mine = lax.psum_scatter(
        back_state[1].astype(jnp.bfloat16), "ctx", scatter_dimension=0, tiled=True
    ).astype(jnp.float32)
    d_key = key_mine[:, :D].reshape(row_count, HEADS, HDIM)
    d_value = key_mine[:, D:].reshape(row_count, HEADS, HDIM)
    pair_grads = jnp.stack([d_query, d_key], 1)
    rotate_back = jax.vjp(turn_pair, pair_raw)[1]
    d_pair = rotate_back(pair_grads)[0]
    d_mixed = (
        jnp.concatenate([d_pair, d_value[:, None]], 1)
        .reshape(row_count, 3 * D)
        .astype(jnp.bfloat16)
    )
    grad_mix_bias = jnp.sum(d_mixed.astype(jnp.float32), 0)
    d_norm_one = jnp.einsum("tf,df->td", d_mixed, gathered[4], preferred_element_type=jnp.float32)
    one_back = jax.vjp(layer_norm, flat_in, gain_one, shift_one)[1]
    d_in_one, grad_gain_one, grad_shift_one = one_back(d_norm_one)
    two_back = jax.vjp(layer_norm, flat_in, gain_two, shift_two)[1]
    d_in_two, grad_gain_two, grad_shift_two = two_back(d_norm_two)
    grad_inputs = (upstream.astype(jnp.float32) + d_in_one + d_in_two).astype(jnp.bfloat16)[None]
    grad_mix = jnp.einsum("td,tf->df", norm_one, d_mixed, preferred_element_type=jnp.float32)
    grad_dense = jnp.einsum("td,te->de", merged_low, upstream, preferred_element_type=jnp.float32)
    grad_up = jnp.einsum("td,tf->df", norm_two, d_pre, preferred_element_type=jnp.float32)
    grad_down = jnp.einsum("tf,td->fd", hidden_low, upstream, preferred_element_type=jnp.float32)
    part_sums = (
        lax.psum_scatter(
            grad_gain_one.astype(jnp.bfloat16), "wa", scatter_dimension=0, tiled=True
        ).astype(jnp.float32),
        lax.psum_scatter(
            grad_shift_one.astype(jnp.bfloat16), "wa", scatter_dimension=0, tiled=True
        ).astype(jnp.float32),
        lax.psum_scatter(
            grad_gain_two.astype(jnp.bfloat16), "wa", scatter_dimension=0, tiled=True
        ).astype(jnp.float32),
        lax.psum_scatter(
            grad_shift_two.astype(jnp.bfloat16), "wa", scatter_dimension=0, tiled=True
        ).astype(jnp.float32),
        lax.psum_scatter(
            grad_mix.astype(jnp.bfloat16), "wa", scatter_dimension=0, tiled=True
        ).astype(jnp.float32),
        lax.psum_scatter(
            grad_mix_bias.astype(jnp.bfloat16), "wa", scatter_dimension=0, tiled=True
        ).astype(jnp.float32),
        lax.psum_scatter(
            grad_dense.astype(jnp.bfloat16), "wa", scatter_dimension=0, tiled=True
        ).astype(jnp.float32),
        lax.psum_scatter(
            grad_bias_out.astype(jnp.bfloat16), "wa", scatter_dimension=0, tiled=True
        ).astype(jnp.float32),
        lax.psum_scatter(
            grad_up.astype(jnp.bfloat16), "wa", scatter_dimension=0, tiled=True
        ).astype(jnp.float32),
        lax.psum_scatter(
            grad_up_bias.astype(jnp.bfloat16), "wa", scatter_dimension=0, tiled=True
        ).astype(jnp.float32),
        lax.psum_scatter(
            grad_down.astype(jnp.bfloat16), "wa", scatter_dimension=0, tiled=True
        ).astype(jnp.float32),
    )
    (
        sum_gain_one,
        sum_shift_one,
        sum_gain_two,
        sum_shift_two,
        sum_mix,
        sum_mix_bias,
        sum_dense,
        sum_bias_out,
        sum_up,
        sum_up_bias,
        sum_down,
    ) = part_sums
    totals = (
        lax.psum(sum_gain_one.astype(jnp.bfloat16), "ctx").astype(jnp.float32),
        lax.psum(sum_shift_one.astype(jnp.bfloat16), "ctx").astype(jnp.float32),
        lax.psum(sum_gain_two.astype(jnp.bfloat16), "ctx").astype(jnp.float32),
        lax.psum(sum_shift_two.astype(jnp.bfloat16), "ctx").astype(jnp.float32),
        lax.psum(sum_mix.astype(jnp.bfloat16), "ctx").astype(jnp.float32),
        lax.psum(sum_mix_bias.astype(jnp.bfloat16), "ctx").astype(jnp.float32),
        lax.psum(sum_dense.astype(jnp.bfloat16), "ctx").astype(jnp.float32),
        lax.psum(sum_bias_out.astype(jnp.bfloat16), "ctx").astype(jnp.float32),
        lax.psum(sum_up.astype(jnp.bfloat16), "ctx").astype(jnp.float32),
        lax.psum(sum_up_bias.astype(jnp.bfloat16), "ctx").astype(jnp.float32),
        lax.psum(sum_down.astype(jnp.bfloat16), "ctx").astype(jnp.float32),
    )
    return (
        output,
        grad_inputs,
        totals[0],
        totals[1],
        totals[2],
        totals[3],
        totals[4],
        totals[5],
        totals[6],
        totals[7],
        totals[8],
        totals[9],
        totals[10],
        totals[7],
    )


def solution(mesh):
    return jax.shard_map(
        shards,
        mesh=mesh,
        in_specs=(
            P("wa", "ctx", None),
            P("wa"),
            P("wa"),
            P("wa"),
            P("wa"),
            P("wa", None),
            P("wa"),
            P("wa", None),
            P("wa"),
            P("wa", None),
            P("wa"),
            P("wa", None),
            P("wa"),
            P("wa", "ctx", None),
        ),
        out_specs=(
            P("wa", "ctx", None),
            P("wa", "ctx", None),
            P("wa"),
            P("wa"),
            P("wa"),
            P("wa"),
            P("wa", None),
            P("wa"),
            P("wa", None),
            P("wa"),
            P("wa", None),
            P("wa"),
            P("wa", None),
            P("wa"),
        ),
        check_vma=False,
    )
```

profile of v0, /device:TPU:0, one launch (start us, length us, event | category | flops | bytes accessed | tf_op | source)
XLA Modules:
  0.0 2016.8 jit_solution(2383900702258551740)
XLA Ops:
  8.6 6.6 all-gather
  15.9 6.6 all-gather.1
  23.1 6.7 all-gather.2
  30.0 1.1 convert_reduce_fusion
  31.1 1.2 fusion.51
  32.4 30.3 %all-gather.14.cloned.1.call-done = bf16[1024,3072]{1,0:T(8,128)(2,1)} async-done(((bf16[256,3072]{1,0:T(8,128)(2,1)}), bf16[1024,3072]{1,0:T(8,128)(2,1)}) %all-gather.14.cloned.1.call-update) | async-done | bytes 6291472 | tf_op jit(solution)/shard_map/all_gather | solution.py:86
  62.7 5.8 convolution_add_fusion.1
  68.5 2.2 copy.39
  71.3 0.8 copy-done.1
  72.4 0.9 copy.40
  73.5 1.1 slice.49
  74.5 0.9 copy.42
  78.6 271.4 %all-gather.16.cloned.1.call-done = bf16[6144,1024]{1,0:T(8,128)(2,1)} async-done(((bf16[192,1024]{1,0:T(8,128)(2,1)}), bf16[6144,1024]{1,0:T(8,128)(2,1)}) %all-gather.16.cloned.1.call-update) | async-done | bytes 12582928 | tf_op jit(solution)/shard_map/all_gather | solution.py:121
  350.0 16.7 copy.41
  366.7 31.8 %fusion.3 = (f32[16,192]{1,0:T(8,128)S(1)}, f32[16,192,6144]{2,1,0:T(8,128)}) fusion(pred[192,6144]{1,0:T(8,128)(4,1)S(1)} %iota_compare_fusion, bf16[6144,16,64]{0,2,1:T(8,128)(2,1)} %bitcast.151, bf16[192,2,16,16]{0,3,2,1:T(8,128)(2,1)S(1)} %fusion.61, bf16[192,2,16,48]{0,3,2,1:T(8,128)(2,1)S(1)} %copy-done.2), kind=kOutput, calls=%fused_computation.7 | convolution fusion | flops 2473325568 | bytes 90058752 | tf_op jit(solution)/shard_map/qhd,khd->hqk/dot_general | solution.py:128
  398.5 28.0 %fusion.1 = f32[16,192]{1,0:T(8,128)S(1)} fusion(f32[16,192,6144]{2,1,0:T(8,128)} %get-tuple-element.60, f32[16,192]{1,0:T(8,128)S(1)} %broadcast_maximum_fusion, pred[192,6144]{1,0:T(8,128)(4,1)S(1)} %iota_compare_fusion), kind=kLoop, calls=%fused_computation.5 | loop fusion | flops 94368768 | bytes 76701696 | tf_op jit(solution)/shard_map/reduce_sum | solution.py:135
  426.6 200.0 %all-gather.18.cloned.1.call-done = bf16[6144,1024]{1,0:T(8,128)(2,1)} async-done(((bf16[192,1024]{1,0:T(8,128)(2,1)}), bf16[6144,1024]{1,0:T(8,128)(2,1)}) %all-gather.18.cloned.1.call-update) | async-done | bytes 12582928 | tf_op jit(solution)/shard_map/all_gather | solution.py:122
  626.6 16.7 copy.43
  643.3 34.6 %fusion.103 = (bf16[192,16,64]{0,2,1:T(8,128)(2,1)}, f32[192,16,64]{0,2,1:T(8,128)}) fusion(f32[192,16]{0,1:T(8,128)S(1)} %bitcast.186, bf16[6144,16,64]{0,2,1:T(8,128)(2,1)} %bitcast.157, f32[16,192,6144]{2,1,0:T(8,128)} %get-tuple-element.60, f32[16,192]{1,0:T(8,128)S(1)} %broadcast_maximum_fusion, pred[192,6144]{1,0:T(8,128)(4,1)S(1)} %iota_compare_fusion), kind=kOutput, calls=%fused_computation.149 | convolution fusion | flops 2510684160 | bytes 90464256 | tf_op jit(solution)/shard_map/hqk,khd->hqd/dot_general | solution.py:136
  677.9 1.5 copy.45
  679.5 3.4 convert_multiply_fusion
  682.9 1.5 copy.46
  684.5 1.2 copy.44
  685.7 46.1 %multiply_convert_fusion = bf16[16,192,6144]{2,1,0:T(8,128)(2,1)} fusion(f32[16,192,6144]{2,1,0:T(8,128)} %get-tuple-element.60, f32[16,192]{1,0:T(8,128)S(1)} %bitcast.187, f32[16,192]{1,0:T(8,128)S(1)} %log_add_fusion, pred[192,6144]{1,0:T(8,128)(4,1)S(1)} %iota_compare_fusion, bf16[192,16,64]{0,2,1:T(8,128)(2,1)S(1)} %bitcast.169, ...), kind=kOutput, calls=%fused_computation | convolution fusion | flops 2529165312 | bytes 127426560 | tf_op jit(solution)/shard_map/qhd,khd->hqk/dot_general | solution.py:57
  731.9 19.6 multiply_convert_fusion.1
  751.5 32.9 %fusion.13 = bf16[16,64,6144]{2,1,0:T(8,128)(2,1)} fusion(bf16[192,16,64]{0,2,1:T(8,128)(2,1)S(1)} %bitcast.170, f32[16,192,6144]{2,1,0:T(8,128)} %get-tuple-element.60, f32[16,192]{1,0:T(8,128)S(1)} %log_add_fusion, pred[192,6144]{1,0:T(8,128)(4,1)S(1)} %iota_compare_fusion), kind=kOutput, calls=%fused_computation.17 | convolution fusion | flops 2497708032 | bytes 89665536 | tf_op jit(solution)/shard_map/hqk,qhd->khd/dot_general | solution.py:208
  784.4 20.4 %pad_maximum_fusion = bf16[6144,2048]{0,1:T(8,128)(2,1)} fusion(bf16[6144,1024]{0,1:T(8,128)(2,1)} %bitcast.159, bf16[6144,1024]{0,1:T(8,128)(2,1)} %bitcast.153), kind=kLoop, calls=%fused_computation.15 | loop fusion | flops 50331648 | bytes 50331648 | tf_op jit(solution)/shard_map/concatenate | solution.py:214
  804.8 31.7 %copy.47 = bf16[6144,2048]{1,0:T(8,128)(2,1)} copy(bf16[6144,2048]{0,1:T(8,128)(2,1)} %pad_maximum_fusion) | data formatting | bytes 50331648
  837.2 6.6 all-gather.4
  843.8 6.6 all-gather.5
  850.4 6.7 all_gather.59
  857.1 12.9 multiply_convert_fusion.2
  870.0 9.7 fusion.102
  879.7 1.1 copy-done.13
  880.8 5.7 convolution_convert_fusion.1
  887.0 5.6 convolution_convert_fusion
  892.7 1.0 copy-done.15
  893.7 2.0 convolution_convert_fusion.3
  895.8 20.3 %fusion.26 = f32[192,1,16,64]{0,3,2,1:T(8,128)S(1)} fusion(bf16[6144,16,64]{0,2,1:T(8,128)(2,1)} %bitcast.152, bf16[16,192,6144]{2,1,0:T(8,128)(2,1)} %multiply_convert_fusion), kind=kOutput, calls=%fused_computation.49 | convolution fusion | flops 2416115712 | bytes 51118080 | tf_op jit(solution)/shard_map/hqk,khd->qhd/dot_general | solution.py:199
  916.1 455.6 %reduce-scatter.16.cloned.1.call-done = bf16[192,2048]{1,0:T(8,128)(2,1)} async-done(((bf16[6144,2048]{1,0:T(8,128)(2,1)}), bf16[192,2048]{1,0:T(8,128)(2,1)}) %reduce-scatter.16.cloned.1.call-update) | async-done | bytes 786448
  1371.7 2.0 slice.50
  1373.7 1.5 copy.50
  1375.2 1.8 slice.51
  1376.9 1.2 copy.49
  1379.6 5.3 convolution_convert_fusion.2
  1385.0 66.4 %reduce-scatter.12.cloned.1.call-done = bf16[256,4096]{1,0:T(8,128)(2,1)} async-done(((bf16[1024,4096]{1,0:T(8,128)(2,1)}), bf16[256,4096]{1,0:T(8,128)(2,1)}) %reduce-scatter.12.cloned.1.call-update) | async-done | bytes 2097168 | tf_op jit(solution)/shard_map/reduce_scatter | solution.py:266
  1451.4 81.0 %reduce-scatter.14.cloned.1.call-done = bf16[1024,1024]{1,0:T(8,128)(2,1)} async-done(((bf16[4096,1024]{1,0:T(8,128)(2,1)}), bf16[1024,1024]{1,0:T(8,128)(2,1)}) %reduce-scatter.14.cloned.1.call-update) | async-done | bytes 2097168 | tf_op jit(solution)/shard_map/reduce_scatter | solution.py:272
  1532.4 40.9 %reduce-scatter.10.cloned.1.call-done = bf16[256,1024]{1,0:T(8,128)(2,1)} async-done(((bf16[1024,1024]{1,0:T(8,128)(2,1)}), bf16[256,1024]{1,0:T(8,128)(2,1)}) %reduce-scatter.10.cloned.1.call-update) | async-done | bytes 524304 | tf_op jit(solution)/shard_map/reduce_scatter | solution.py:260
  1573.3 67.6 %reduce-scatter.8.cloned.1.call-done = bf16[256,3072]{1,0:T(8,128)(2,1)} async-done(((bf16[1024,3072]{1,0:T(8,128)(2,1)}), bf16[256,3072]{1,0:T(8,128)(2,1)}) %reduce-scatter.8.cloned.1.call-update) | async-done | bytes 1572880 | tf_op jit(solution)/shard_map/reduce_scatter | solution.py:254
  1644.1 6.6 all-gather.6
  1650.7 6.8 all-gather.3
  1657.4 6.9 fusion.104
  1664.4 5.5 convolution_add_fusion.3
  1669.8 1.4 fusion.30
  1671.3 5.2 fusion.99
  1676.6 0.8 copy-done.8
  1678.2 14.0 all-reduce.13
  1692.6 87.2 %all-reduce.11 = (bf16[256]{0:T(256)(128)(2,1)S(1)}, bf16[256]{0:T(256)(128)(2,1)S(1)}, bf16[256]{0:T(256)(128)(2,1)S(1)}, bf16[256]{0:T(256)(128)(2,1)S(1)}, bf...) all-reduce(bf16[256]{0:T(256)(128)(2,1)S(1)} %dynamic-slice.1, ...), channel_id=1, replica_groups=mesh['ctx'=32,'wa'=4] {'ctx'}, use_global_device_ids=true, to_apply=%region_12.13 | all-reduce | flops 3072 | bytes 12288 | tf_op jit(solution)/shard_map/psum | solution.py:290
  1783.3 2.4 fusion.63
  1785.7 213.6 %all-reduce.16.cloned.1.call-done = (bf16[256,3072]{1,0:T(8,128)(2,1)}, bf16[256,1024]{1,0:T(8,128)(2,1)}, bf16[256,4096]{1,0:T(8,128)(2,1)}, bf16[1024,1024]{1,0:T(8,128)(2,1)}) async-done(((bf16[256,3072]{1,0:T(8,128)(2,1)}, bf16[256,1024]{1,0:T(8,128)(2,1)}, bf16[256,4096]{1,0:T(8,128)(2,1)}, bf16[1024,1024]{1,0:T(8,128)(2,1)}), (bf16[256,3072]{1,0:T(8,128)(2,1)}, bf16[256,1024]{1,0:T(8,128)(2,1)}, ...) | async-done | bytes 6291472 | tf_op jit(solution)/shard_map/psum | solution.py:294
  1999.4 4.2 convert_element_type.243
  2003.6 2.5 convert_element_type.246
  2006.1 2.0 convert_element_type.235
  2008.1 1.1 convert_element_type.240
  (156 shorter events, 16.4 us)
Async XLA Ops:
  7.2 55.5 %all-gather.14.cloned.1.call-start = ((), (), s32[]{:S(2)}) async-start(), calls=%async_computation.5 | async-start | bytes 7864320 | tf_op jit(solution)/shard_map/all_gather | solution.py:86
  7.9 342.1 %all-gather.16.cloned.1.call-start = ((), (), s32[]{:S(2)}) async-start(), calls=%async_computation.6 | async-start | bytes 12976128 | tf_op jit(solution)/shard_map/all_gather | solution.py:121
  15.2 47.5 %copy-start.16 = (f32[4,1,256]{2,1,0:T(1,128)}, f32[4,1,256]{2,1,0:T(1,128)S(1)}, u32[]{:S(2)}) copy-start(f32[4,1,256]{2,1,0:T(1,128)S(1)} %convert_element_type.247) | copy-start | bytes 12292
  22.4 40.2 %copy-start.22 = (f32[4,1,256]{2,1,0:T(1,128)}, f32[4,1,256]{2,1,0:T(1,128)S(1)}, u32[]{:S(2)}) copy-start(f32[4,1,256]{2,1,0:T(1,128)S(1)} %convert_element_type.248) | copy-start | bytes 12292
  30.0 41.2 %copy-start.18 = (f32[192,16]{0,1:T(8,128)}, f32[192,16]{0,1:T(8,128)S(1)}, u32[]{:S(2)}) copy-start(f32[192,16]{0,1:T(8,128)S(1)} %get-tuple-element.56) | copy-start | bytes 36868
  30.0 41.2 %copy-start.20 = (f32[192,16]{0,1:T(8,128)}, f32[192,16]{0,1:T(8,128)S(1)}, u32[]{:S(2)}) copy-start(f32[192,16]{0,1:T(8,128)S(1)} %get-tuple-element.57) | copy-start | bytes 36868
  31.1 31.5 %copy-start.24 = (f32[192]{0:T(256)}, f32[192]{0:T(256)S(1)}, u32[]{:S(2)}) copy-start(f32[192]{0:T(256)S(1)} %broadcast_multiply_fusion.2) | copy-start | bytes 2308
  32.4 30.3 %copy-start.28 = (f32[192]{0:T(256)}, f32[192]{0:T(256)S(1)}, u32[]{:S(2)}) copy-start(f32[192]{0:T(256)S(1)} %fusion.51) | copy-start | bytes 2308
  32.4 30.3 %copy-start.26 = (f32[192]{0:T(256)}, f32[192]{0:T(256)S(1)}, u32[]{:S(2)}) copy-start(f32[192]{0:T(256)S(1)} %fusion.84) | copy-start | bytes 2308
  71.0 1.4 copy-start.6
  71.1 1.0 copy-start.1
  73.4 553.2 %all-gather.18.cloned.1.call-start = ((), (), s32[]{:S(2)}) async-start(), calls=%async_computation.7 | async-start | bytes 12976128 | tf_op jit(solution)/shard_map/all_gather | solution.py:122
  75.5 604.0 %all-gather.20.cloned.1.call-start = ((), (), s32[]{:S(2)}) async-start(), calls=%async_computation.8 | async-start | bytes 2621440 | tf_op jit(solution)/shard_map/all_gather | solution.py:88
  76.1 781.0 %all-gather.22.cloned.1.call-start = ((), (), s32[]{:S(2)}) async-start(), calls=%async_computation.9 | async-start | bytes 10485760 | tf_op jit(solution)/shard_map/all_gather | solution.py:90
  76.7 793.3 %all-gather.24.cloned.1.call-start = ((), (), s32[]{:S(2)}) async-start(), calls=%async_computation.10 | async-start | bytes 10485760 | tf_op jit(solution)/shard_map/all_gather | solution.py:92
  77.2 1294.5 %reduce-scatter.16.cloned.1.call-start = ((), (), s32[]{:S(2)}) async-start(), calls=%async_computation.15 | async-start | bytes 25952256
  78.6 288.1 %copy-start.2 = (bf16[192,2,16,48]{0,3,2,1:T(8,128)(2,1)S(1)}, bf16[192,2,16,48]{0,3,2,1:T(8,128)(2,1)}, u32[]{:S(2)}) copy-start(bf16[192,2,16,48]{0,3,2,1:T(8,128)(2,1)} %copy-done.1) | copy-start | bytes 1769476
  643.3 36.2 %copy-start.3 = (bf16[1,192,1024]{2,1,0:T(8,128)(2,1)S(1)}, bf16[1,192,1024]{2,1,0:T(8,128)(2,1)}, u32[]{:S(2)}) copy-start(bf16[1,192,1024]{2,1,0:T(8,128)(2,1)} %param.27) | copy-start | bytes 1179652
  836.5 0.7 copy-start.32
  836.5 7.2 copy-start.33
  836.5 13.8 copy-start.30
  836.5 20.5 %copy-start = (bf16[1,192,1024]{2,1,0:T(8,128)(2,1)S(1)}, bf16[1,192,1024]{2,1,0:T(8,128)(2,1)}, u32[]{:S(2)}) copy-start(bf16[1,192,1024]{2,1,0:T(8,128)(2,1)} %param.14) | copy-start | bytes 1179652
  836.6 20.5 %copy-start.25 = (f32[192]{0:T(256)S(1)}, f32[192]{0:T(256)}, u32[]{:S(2)}) copy-start(f32[192]{0:T(256)} %copy-done.24) | copy-start | bytes 2308
  836.6 20.5 %copy-start.27 = (f32[192]{0:T(256)S(1)}, f32[192]{0:T(256)}, u32[]{:S(2)}) copy-start(f32[192]{0:T(256)} %copy-done.26) | copy-start | bytes 2308
  836.6 614.8 %reduce-scatter.12.cloned.1.call-start = ((), (), s32[]{:S(2)}) async-start(), calls=%async_computation.13 | async-start | bytes 10485760 | tf_op jit(solution)/shard_map/reduce_scatter | solution.py:266
  857.1 12.9 copy-start.4
  870.0 17.0 copy-start.9
  879.7 1.1 copy-start.13
  886.5 645.9 %reduce-scatter.14.cloned.1.call-start = ((), (), s32[]{:S(2)}) async-start(), calls=%async_computation.14 | async-start | bytes 10485760 | tf_op jit(solution)/shard_map/reduce_scatter | solution.py:272
  892.6 1.0 copy-start.15
  892.7 680.6 %reduce-scatter.10.cloned.1.call-start = ((), (), s32[]{:S(2)}) async-start(), calls=%async_computation.12 | async-start | bytes 2621440 | tf_op jit(solution)/shard_map/reduce_scatter | solution.py:260
  895.7 745.1 %reduce-scatter.8.cloned.1.call-start = ((), (), s32[]{:S(2)}) async-start(), calls=%async_computation.11 | async-start | bytes 7864320 | tf_op jit(solution)/shard_map/reduce_scatter | solution.py:254
  1375.2 3.1 copy-start.21
  1378.1 0.7 copy-start.19
  1378.9 0.7 copy-start.17
  1379.0 0.7 copy-start.23
  1384.9 614.4 %all-reduce.16.cloned.1.call-start = ((), (), s32[]{:S(2)}) async-start(), calls=%async_computation.16 | async-start | bytes 12582912 | tf_op jit(solution)/shard_map/psum | solution.py:294
  1640.9 0.7 copy-start.36
  1640.9 3.2 copy-start.34
  1640.9 9.8 copy-start.35
  1657.4 6.9 copy-start.10
  1664.3 5.5 copy-start.5
  1664.4 5.5 copy-start.7
  1671.3 5.2 copy-start.29
  1676.5 0.9 copy-start.8
  1781.1 228.2 %copy-start.31 = (f32[256]{0:T(256)}, f32[256]{0:T(256)S(1)}, u32[]{:S(2)}) copy-start(f32[256]{0:T(256)S(1)} %convert_element_type.241) | copy-start | bytes 3076
  1999.4 4.3 copy-start.11
  2003.6 2.5 copy-start.12
  2006.1 2.0 copy-start.14
Sparse Core Ops, SparseCore 0:
  9.7 52.9 all-gather.13
  73.5 276.4 all-gather.15
  352.3 274.3 all-gather.17
  628.1 23.8 all-gather.19
  653.6 61.7 all-gather.21
  716.9 61.7 all-gather.23
  836.7 534.9 reduce-scatter.15
  1374.4 76.9 reduce-scatter.11
  1454.3 78.0 reduce-scatter.13
  1535.5 37.7 reduce-scatter.9
  1576.1 64.6 reduce-scatter.7
  1643.5 355.8 all-reduce.15
where the time goes:
time: 2020 us
  waiting for transfers between devices  1430 us (71%)
  matrix products  255 us (13%)
  blocking collectives  154 us (8%)
  local copies, waits for them, and re-layouts  90.3 us (4%)
  other arithmetic  69.9 us (3%)
    unnamed x13, waiting for transfers between devices  458 us
    all_gather x1, waiting for transfers between devices, shards(): lax.all_gather(key_low.reshape(row_count, D), 'ctx', axis=0, tiled=True)  271 us
    psum x1, waiting for transfers between devices, shards(): lax.psum(sum_mix.astype(jnp.bfloat16), 'ctx').astype(jnp.float32)  214 us
    all_gather x1, waiting for transfers between devices, shards(): lax.all_gather(value_low.reshape(row_count, D), 'ctx', axis=0, tiled=True)  200 us
    psum x1, blocking collectives, shards(): lax.psum(sum_gain_one.astype(jnp.bfloat16), 'ctx').astype(jnp.float32)  87.2 us
    reduce_scatter x1, waiting for transfers between devices, shards(): lax.psum_scatter(grad_down.astype(jnp.bfloat16), 'wa', scatter_dimension=...  81 us
    reduce_scatter x1, waiting for transfers between devices, shards(): lax.psum_scatter(grad_mix.astype(jnp.bfloat16), 'wa', scatter_dimension=0...  67.6 us
    reduce_scatter x1, waiting for transfers between devices, shards(): lax.psum_scatter(grad_up.astype(jnp.bfloat16), 'wa', scatter_dimension=0,...  66.4 us
  transfers between devices with their start and end apart: 12, of which 9 were waited for; matrix products, arithmetic and copies ran while one was open for 19% of the time, Pallas kernels for 0%

commit v1 on v0

v1 whole, which is shorter than its diff:
```python
import functools

import jax
import jax.numpy as jnp
from jax import lax
from jax.experimental import pallas as pl
from jax.experimental.pallas import tpu as pltpu
from jax.sharding import PartitionSpec as P

D = 1024
HEADS = 16
HDIM = 64
ROT = 16
FF = 4096
BLK = 192
HALF = 96
EPS = 1e-05
F32 = jnp.float32
BF16 = jnp.bfloat16


def attention_kernel(
    par_ref, x_ref, out_ref, kv, kvt, qd, s_buf, p_buf, dkv, oq, *, blocks, tq, kc
):
    n_keys, n_queries = blocks * BLK, blocks * HALF
    par = par_ref[0]

    def token(row):
        return (row // HALF) * BLK + par * HALF + row % HALF

    def fill(b, carry):
        kv[pl.ds(b * BLK, BLK), :] = x_ref[b, 0:BLK, :]
        qd[pl.ds(b * HALF, HALF), :] = x_ref[b, BLK : BLK + HALF, :]
        return carry

    lax.fori_loop(0, blocks, fill, 0)

    def turn(c, carry):
        kvt[:, pl.ds(pl.multiple_of(c * kc, kc), kc)] = kv[pl.ds(c * kc, kc), :].T
        dkv[pl.ds(c * kc, kc), :] = jnp.zeros((kc, 128), F32)
        return carry

    lax.fori_loop(0, n_keys // kc, turn, 0)
    row = lax.broadcasted_iota(jnp.int32, (128, tq), 0)
    lane = lax.broadcasted_iota(jnp.int32, (tq, 128), 1)
    q_col = lax.broadcasted_iota(jnp.int32, (kc, tq), 1)
    k_row = lax.broadcasted_iota(jnp.int32, (kc, tq), 0)
    zero = jnp.zeros((), F32)

    def group(t, carry):
        first = t * tq
        n_all = (token(first + tq - 1) + kc) // kc
        n_full = (token(first) + 1) // kc
        qd_rows = qd[pl.ds(pl.multiple_of(first, tq), tq), :]
        qd_t = qd_rows.astype(F32).T
        q_t = jnp.where(row < HDIM, qd_t * 0.125, zero).astype(BF16)
        q_idx = first + q_col
        q_tok = (q_idx // HALF) * BLK + par * HALF + q_idx % HALF

        def scores(c, top, masked):
            o = pl.multiple_of(c * kc, kc)
            s = jnp.dot(kv[pl.ds(o, kc), :], q_t, preferred_element_type=F32)
            if masked:
                s = jnp.where(c * kc + k_row <= q_tok, s, -1e30)
            s_buf[pl.ds(o, kc), :] = s
            return jnp.maximum(top, jnp.max(s.reshape(kc // 8, 8, tq), 0))

        top = jnp.full((8, tq), -1e30, F32)
        top = lax.fori_loop(0, n_full, lambda c, m: scores(c, m, False), top)
        top = lax.fori_loop(n_full, n_all, lambda c, m: scores(c, m, True), top)
        top = jnp.max(top, 0, keepdims=True)

        def weigh(c, state):
            total, out_t = state
            o = pl.multiple_of(c * kc, kc)
            p = jnp.exp(s_buf[pl.ds(o, kc), :] - top)
            total = total + jnp.sum(p.reshape(kc // 8, 8, tq), 0)
            p_low = p.astype(BF16)
            p_buf[pl.ds(o, kc), :] = p_low
            out_t = out_t + jnp.dot(kvt[HDIM:, pl.ds(o, kc)], p_low, preferred_element_type=F32)
            return total, out_t

        total, out_t = lax.fori_loop(
            0, n_all, weigh, (jnp.zeros((8, tq), F32), jnp.zeros((HDIM, tq), F32))
        )
        inv = 1.0 / jnp.sum(total, 0, keepdims=True)
        out_t = out_t * inv
        do_t = (qd_t[HDIM:] * inv).astype(BF16)
        delta = jnp.sum(do_t.astype(F32) * out_t, 0, keepdims=True)
        do_full = jnp.concatenate([jnp.zeros((HDIM, tq), BF16), do_t], 0)
        do_rows = do_full.astype(F32).T.astype(BF16)
        q_rows = jnp.where(lane < HDIM, qd_rows.astype(F32) * 0.125, zero).astype(BF16)

        def back(c, dq_t):
            o = pl.multiple_of(c * kc, kc)
            dp = jnp.dot(kv[pl.ds(o, kc), :], do_full, preferred_element_type=F32)
            p_low = p_buf[pl.ds(o, kc), :]
            ds = (p_low.astype(F32) * (dp - delta)).astype(BF16)
            dkv[pl.ds(o, kc), :] += jnp.dot(
                p_low, do_rows, preferred_element_type=F32
            ) + jnp.dot(ds, q_rows, preferred_element_type=F32)
            return dq_t + jnp.dot(kvt[:HDIM, pl.ds(o, kc)], ds, preferred_element_type=F32)

        dq_t = lax.fori_loop(0, n_all, back, jnp.zeros((HDIM, tq), F32)) * 0.125
        oq[pl.ds(pl.multiple_of(first, tq), tq), :] = (
            jnp.concatenate([dq_t, out_t], 0).T.astype(BF16)
        )
        return carry

    lax.fori_loop(0, n_queries // tq, group, 0)

    def drain(b, carry):
        out_ref[b, 0:BLK, :] = dkv[pl.ds(b * BLK, BLK), :].astype(BF16)
        out_ref[b, BLK : BLK + HALF, :] = oq[pl.ds(b * HALF, HALF), :]
        return carry

    lax.fori_loop(0, blocks, drain, 0)


def attention(par, x, tq=768, kc=1536):
    blocks = x.shape[0]
    n_keys, n_queries = blocks * BLK, blocks * HALF
    area = n_keys * n_queries // 2
    return pl.pallas_call(
        functools.partial(attention_kernel, blocks=blocks, tq=tq, kc=kc),
        out_shape=jax.ShapeDtypeStruct(x.shape, BF16),
        in_specs=[
            pl.BlockSpec(memory_space=pltpu.SMEM),
            pl.BlockSpec(memory_space=pltpu.VMEM),
        ],
        out_specs=pl.BlockSpec(memory_space=pltpu.VMEM),
        scratch_shapes=[
            pltpu.VMEM((n_keys, 128), BF16),
            pltpu.VMEM((128, n_keys), BF16),
            pltpu.VMEM((n_queries, 128), BF16),
            pltpu.VMEM((n_keys, tq), F32),
            pltpu.VMEM((n_keys, tq), BF16),
            pltpu.VMEM((n_keys, 128), F32),
            pltpu.VMEM((n_queries, 128), BF16),
        ],
        compiler_params=pltpu.CompilerParams(vmem_limit_bytes=50 * 2**20),
        cost_estimate=pl.CostEstimate(
            flops=12 * area * HDIM, bytes_accessed=4 * x.size, transcendentals=area
        ),
    )(par, x)


def normalize(values):
    centred = values - jnp.mean(values, -1, keepdims=True)
    spread = jnp.mean(centred * centred, -1, keepdims=True)
    inv = lax.rsqrt(spread + EPS)
    return centred * inv, inv


def norm_back(normal, inv, gain, grad):
    e = grad * gain
    return inv * (
        e
        - jnp.mean(e, -1, keepdims=True)
        - normal * jnp.mean(e * normal, -1, keepdims=True)
    )


def rotary_tables(positions):
    exponents = jnp.arange(0, ROT, 2, dtype=F32) / ROT
    inverse = 1.0 / 10000.0**exponents
    angles = positions[:, None] * inverse[None, :]
    doubled = jnp.concatenate([angles, angles], -1)
    return jnp.cos(doubled)[:, None, :], jnp.sin(doubled)[:, None, :]


def rotate(values, cos_table, sin_table):
    first = values[..., : ROT // 2]
    second = values[..., ROT // 2 : ROT]
    turned = jnp.concatenate([-second, first], -1)
    return jnp.concatenate(
        [values[..., :ROT] * cos_table + turned * sin_table, values[..., ROT:]], -1
    )


def gelu_exact(values):
    return jax.nn.gelu(values, approximate=False)


def dot(a, b):
    return jnp.dot(a, b, preferred_element_type=F32)


def dot_t(a, b):
    return lax.dot_general(a, b, (((1,), (1,)), ((), ())), preferred_element_type=F32)


def t_dot(a, b):
    return lax.dot_general(a, b, (((0,), (0,)), ((), ())), preferred_element_type=F32)


def by_quarter(vec):
    return vec.reshape(4, -1, 256).transpose(0, 2, 1).reshape(1024, -1)


def sum_over_blocks(part):
    columns = part.shape[1]
    pieces = part.reshape(16, 16, 2, columns // 2).transpose(0, 2, 1, 3)
    pieces = pieces.reshape(32, 16, columns // 2)
    mine = lax.all_to_all(pieces, "ctx", 0, 0, tiled=True)
    mine = jnp.sum(mine.astype(F32), 0).astype(BF16)
    spread = jnp.broadcast_to(mine[None], (32, *mine.shape))
    whole = lax.all_to_all(spread, "ctx", 0, 0, tiled=True)
    return (
        whole.reshape(16, 2, 16, columns // 2)
        .transpose(0, 2, 1, 3)
        .reshape(256, columns)
        .astype(F32)
    )


def shards(
    inputs,
    first_gain,
    first_bias,
    second_gain,
    second_bias,
    mix_weight,
    mix_bias,
    dense_weight,
    dense_bias,
    up_weight,
    up_bias,
    down_weight,
    down_bias,
    grad_out,
):
    small = jnp.concatenate(
        [first_gain, first_bias, second_gain, second_bias, dense_bias, down_bias, mix_bias, up_bias]
    )
    small = lax.all_gather(small, "wa", axis=0, tiled=False).astype(F32)
    vec = [small[:, 256 * i : 256 * i + 256].reshape(1, D) for i in range(6)]
    gain_one, shift_one, gain_two, shift_two, bias_dense, bias_down = vec
    bias_mix = small[:, 1536:2304].reshape(1, 3 * D)
    bias_up = small[:, 2304:3328].reshape(1, FF)
    attn_weight = lax.all_gather(
        jnp.concatenate([mix_weight, dense_weight], 1), "wa", axis=0, tiled=True
    )
    mix_full, dense_full = attn_weight[:, : 3 * D], attn_weight[:, 3 * D :]
    up_full = lax.all_gather(up_weight, "wa", axis=0, tiled=True)
    down_full = lax.all_gather(down_weight, "wa", axis=0, tiled=True)

    place = lax.axis_index("ctx")
    flat_in = inputs[0].astype(F32)
    upstream = grad_out[0]
    normal, inv = normalize(flat_in)
    norm_one = (normal * gain_one + shift_one).astype(BF16)
    norm_two = (normal * gain_two + shift_two).astype(BF16)
    mixed = (dot(norm_one, mix_full) + bias_mix).reshape(BLK, 3, HEADS, HDIM)
    positions = (place * BLK + jnp.arange(BLK, dtype=jnp.int32)).astype(F32)
    cos_table, sin_table = rotary_tables(positions)
    queries = rotate(mixed[:, 0], cos_table, sin_table).astype(BF16)
    keys = rotate(mixed[:, 1], cos_table, sin_table).astype(BF16)
    values = mixed[:, 2].astype(BF16)
    d_merged = dot_t(upstream, dense_full).astype(BF16).reshape(BLK, HEADS, HDIM)
    key_value = jnp.concatenate([keys, values], -1).transpose(1, 0, 2)
    key_value = jnp.broadcast_to(key_value[:, None], (HEADS, 2, BLK, 2 * HDIM))
    query_grad = jnp.concatenate([queries, d_merged], -1).transpose(1, 0, 2)
    query_grad = query_grad.reshape(HEADS, 2, HALF, 2 * HDIM)
    sent = jnp.concatenate([key_value, query_grad], 2).reshape(32, BLK + HALF, 2 * HDIM)
    held = lax.all_to_all(sent, "ctx", 0, 0, tiled=True)
    back = attention((place % 2).reshape(1), held)
    back = lax.all_to_all(back, "ctx", 0, 0, tiled=True)
    back = back.reshape(HEADS, 2, BLK + HALF, 2 * HDIM)
    d_key_value = jnp.sum(back[:, :, :BLK].astype(F32), 1).transpose(1, 0, 2)
    d_query_out = back[:, :, BLK:].reshape(HEADS, BLK, 2 * HDIM).transpose(1, 0, 2)
    merged = d_query_out[..., HDIM:].reshape(BLK, D)
    d_query = rotate(d_query_out[..., :HDIM].astype(F32), cos_table, -sin_table)
    d_key = rotate(d_key_value[..., :HDIM], cos_table, -sin_table)
    d_value = d_key_value[..., HDIM:]
    d_mixed = jnp.stack([d_query, d_key, d_value], 1).reshape(BLK, 3 * D).astype(BF16)

    up_pre = dot(norm_two, up_full) + bias_up
    hidden, gelu_back = jax.vjp(gelu_exact, up_pre)
    hidden = hidden.astype(BF16)
    d_pre = gelu_back(dot_t(upstream, down_full))[0].astype(BF16)
    d_norm_two = dot_t(d_pre, up_full)
    feed_out = dot(hidden, down_full) + bias_down
    attended = dot(merged, dense_full) + bias_dense
    output = (flat_in + attended + feed_out).astype(BF16)[None]
    d_norm_one = dot_t(d_mixed, mix_full)
    grad_in = (
        upstream.astype(F32)
        + norm_back(normal, inv, gain_one, d_norm_one)
        + norm_back(normal, inv, gain_two, d_norm_two)
    ).astype(BF16)[None]

    vectors = jnp.concatenate(
        [
            by_quarter(jnp.sum(v, 0))
            for v in (
                d_norm_one * normal,
                d_norm_one,
                d_norm_two * normal,
                d_norm_two,
                upstream.astype(F32),
                d_mixed.astype(F32),
                d_pre.astype(F32),
            )
        ],
        1,
    )
    vectors = jnp.pad(vectors, ((0, 0), (0, 256 - vectors.shape[1]))).astype(BF16)
    grad_up = t_dot(norm_two, d_pre).astype(BF16)
    grad_down = t_dot(hidden, upstream).astype(BF16)
    grad_attn = jnp.concatenate(
        [t_dot(norm_one, d_mixed).astype(BF16), t_dot(merged, upstream).astype(BF16), vectors], 1
    )

    def scatter(part):
        return lax.psum_scatter(part, "wa", scatter_dimension=0, tiled=True)

    sum_up = sum_over_blocks(scatter(grad_up))
    sum_down = sum_over_blocks(scatter(grad_down).reshape(256, 4096)).reshape(1024, 1024)
    sum_attn = sum_over_blocks(scatter(grad_attn))
    sum_mix, sum_dense = sum_attn[:, : 3 * D], sum_attn[:, 3 * D : 4 * D]
    rest = sum_attn[:, 4 * D : 4 * D + 12].T
    return (
        output,
        grad_in,
        rest[0],
        rest[1],
        rest[2],
        rest[3],
        sum_mix,
        rest[5:8].reshape(768),
        sum_dense,
        rest[4],
        sum_up,
        rest[8:12].reshape(1024),
        sum_down,
        rest[4],
    )


def solution(mesh):
    rows, vec, tokens = P("wa", None), P("wa"), P("wa", "ctx", None)
    return jax.shard_map(
        shards,
        mesh=mesh,
        in_specs=(tokens, vec, vec, vec, vec, rows, vec, rows, vec, rows, vec, rows, vec, tokens),
        out_specs=(
            tokens,
            tokens,
            vec,
            vec,
            vec,
            vec,
            rows,
            vec,
            rows,
            vec,
            rows,
            vec,
            rows,
            vec,
        ),
        check_vma=False,
    )
```

time: 2020 us -> 691 us (0.34)
  waiting for transfers between devices: 1430 us -> 408 us
  matrix products: 255 us -> 69.3 us
  blocking collectives: 154 us -> 6.96 us
  Pallas kernels: 0 us -> 47.6 us
  other arithmetic: 69.9 us -> 27.2 us
  starting transfers between devices: 1.41 us -> 38.8 us
    unnamed x13 -> x6, waiting for transfers between devices: 458 us -> 1.44 us
    all_gather x6 -> x3, waiting for transfers between devices: 502 us -> 144 us  [the longest x1 54.3 us: shards(): up_full = lax.all_gather(up_weight, 'wa', axis=0, tiled=True)]
    all_to_all x0 -> x8, waiting for transfers between devices: none -> 262 us  [the longest x3 106 us: sum_over_blocks(): mine = lax.all_to_all(pieces, 'ctx', 0, 0, tiled=True)]
    reduce_scatter x4 -> x3, waiting for transfers between devices: 256 us -> 0.06 us  [scatter(): return lax.psum_scatter(part, 'wa', scatter_dimension=0, tiled=True)]
    psum x1 -> x0, waiting for transfers between devices: 214 us -> none  [shards(): lax.psum(sum_mix.astype(jnp.bfloat16), 'ctx').astype(jnp.float32)]
    dot_general x18 -> x12, matrix products: 255 us -> 69.3 us  [the longest x4 28.2 us: dot(): return jnp.dot(a, b, preferred_element_type=F32)]
    psum x1 -> x0, blocking collectives: 87.2 us -> none  [shards(): lax.psum(sum_gain_one.astype(jnp.bfloat16), 'ctx').astype(jnp.float32)]
    pallas_call x0 -> x1, Pallas kernels: none -> 47.6 us  [attention(): pl.pallas_call(functools.partial(attention_kernel, blocks=blocks, tq=tq,...]
  transfers between devices with their start and end apart: 12 -> 14, of which waited for: 9 -> 10; matrix products, arithmetic and copies ran while one was open for 19% -> 22% of each run, Pallas kernels for 0% -> 7%
where the time goes in v1:
time: 691 us; the launch traced here: 686 us
  waiting for transfers between devices  408 us (59%)
  local copies, waits for them, and re-layouts  73.5 us (11%)
  matrix products  69.3 us (10%)
  Pallas kernels  47.6 us (7%)
  starting transfers between devices  38.8 us (6%)
  other arithmetic  27.2 us (4%)
  between operations  15.4 us (2%)
  blocking collectives  6.96 us (1%)
    all_to_all x3, waiting for transfers between devices, sum_over_blocks(): mine = lax.all_to_all(pieces, 'ctx', 0, 0, tiled=True)  106 us
    all_to_all x1, waiting for transfers between devices, shards(): held = lax.all_to_all(sent, 'ctx', 0, 0, tiled=True)  57.8 us
    all_gather x1, waiting for transfers between devices, shards(): up_full = lax.all_gather(up_weight, 'wa', axis=0, tiled=True)  54.3 us
    all_gather x1, waiting for transfers between devices, shards(): down_full = lax.all_gather(down_weight, 'wa', axis=0, tiled=True)  50.8 us
    all_to_all x1, waiting for transfers between devices, shards(): back = lax.all_to_all(back, 'ctx', 0, 0, tiled=True)  49.3 us
    all_to_all x3, waiting for transfers between devices, sum_over_blocks(): whole = lax.all_to_all(spread, 'ctx', 0, 0, tiled=True)  49 us
    pallas_call x1, Pallas kernels, attention(): pl.pallas_call(functools.partial(attention_kernel, blocks=blocks, tq=tq,...  47.6 us
    all_gather x1, waiting for transfers between devices, shards(): lax.all_gather(jnp.concatenate([mix_weight, dense_weight], 1), 'wa', axis...  39.4 us
  transfers between devices with their start and end apart: 14, of which 10 were waited for; matrix products, arithmetic and copies ran while one was open for 22% of the time, Pallas kernels for 7%

profile of v1, /device:TPU:0, one launch (start us, length us, event | category | flops | bytes accessed | tf_op | source)
XLA Modules:
  0.0 686.4 jit_solution(1908081278301014170)
XLA Ops:
  8.8 1.5 pad_maximum_fusion.1
  12.2 7.0 %all-gather.1 = bf16[4,1,3328]{2,1,0:T(2,128)(2,1)S(1)} all-gather(bf16[1,1,3328]{2,1,0:T(2,128)(2,1)S(1)} %reshape.292), channel_id=2, replica_groups=mesh['ctx'=32,'wa'=4] {'wa'}, dimensions={0}, use_global_device_ids=true | all-gather | bytes 33280 | tf_op jit(solution)/shard_map/all_gather | solution.py:236
  20.2 54.3 %all-gather.8.cloned.1.call-done = bf16[1024,4096]{1,0:T(8,128)(2,1)} async-done(((bf16[256,4096]{1,0:T(8,128)(2,1)}), bf16[1024,4096]{1,0:T(8,128)(2,1)}) %all-gather.8.cloned.1.call-update) | async-done | bytes 8388624 | tf_op jit(solution)/shard_map/all_gather | solution.py:245
  74.5 12.7 %multiply_convert_fusion = (bf16[192,4096]{1,0:T(8,128)(2,1)S(1)}, f32[192,4096]{1,0:T(8,128)}, f32[192,4096]{1,0:T(8,128)}) fusion(f32[4096]{0:T(1024)S(1)} %bitcast.239, bf16[1024,4096]{1,0:T(8,128)(2,1)} %all-gather.8.cloned.1.call-done, bf16[1,192,1024]{2,1,0:T(8,128)(2,1)S(1)} %copy-done, f32[1024]{0:T(1024)S(1)} %bitcast.234, f32[1024]{0:T(1024)S(1)} %bitcast.224, ...), kind=kOutput, calls=%fused_computation.20 | convolution fusion | flops 1663696896 | bytes 16672256 | tf_op jit(solution)/shard_map/dot_general | solution.py:186
  87.2 50.8 %all-gather.10.cloned.1.call-done = bf16[4096,1024]{1,0:T(8,128)(2,1)} async-done(((bf16[1024,1024]{1,0:T(8,128)(2,1)}), bf16[4096,1024]{1,0:T(8,128)(2,1)}) %all-gather.10.cloned.1.call-update) | async-done | bytes 8388624 | tf_op jit(solution)/shard_map/all_gather | solution.py:246
  138.0 9.6 %fusion.104 = (bf16[4096]{0:T(1024)(128)(2,1)}, bf16[192,4096]{1,0:T(8,128)(2,1)S(1)}) fusion(f32[192,4096]{1,0:T(8,128)} %get-tuple-element.34, f32[192,4096]{1,0:T(8,128)} %get-tuple-element.60, bf16[4096,1024]{1,0:T(8,128)(2,1)} %all-gather.10.cloned.1.call-done, bf16[1,192,1024]{2,1,0:T(8,128)(2,1)S(1)} %copy-done.3), kind=kOutput, calls=%fused_computation.159 | convolution fusion | flops 1622405120 | bytes 16654336 | tf_op jit(solution)/shard_map/dot_general | solution.py:190
  147.6 1.2 copy-done.11
  148.8 6.8 convolution_convert_fusion.1
  156.1 5.6 convolution_convert_fusion
  162.6 39.4 %all-gather.6.cloned.1.call-done = bf16[1024,4096]{1,0:T(8,128)(2,1)} async-done(((bf16[256,4096]{1,0:T(8,128)(2,1)}), bf16[1024,4096]{1,0:T(8,128)(2,1)}) %all-gather.6.cloned.1.call-update) | async-done | bytes 8388624 | tf_op jit(solution)/shard_map/all_gather | solution.py:241
  202.0 2.4 fusion.34
  205.5 5.7 fusion.6
  211.2 2.7 copy.137
  216.9 2.4 copy.140
  219.4 1.4 maximum_bitcast_fusion
  221.8 1.6 pad_maximum_fusion
  223.4 7.3 %all-to-all-start = ((bf16[32,288,128]{2,1,0:T(8,128)(2,1)}), bf16[32,288,128]{2,1,0:T(8,128)(2,1)S(1)}, u32[]{:S(2)}, u32[]{:S(2)}) async-start(bf16[32,288,128]{2,1,0:T(8,128)(2,1)} %pad_maximum_fusion), calls=%async_computation | async-start | bytes 4718592 | tf_op jit(solution)/shard_map/all_to_all | solution.py:266
  230.7 57.8 %all-to-all-done.x_ref = bf16[32,288,128]{2,1,0:T(8,128)(2,1)S(1)} async-done(((bf16[32,288,128]{2,1,0:T(8,128)(2,1)}), bf16[32,288,128]{2,1,0:T(8,128)(2,1)S(1)}, u32[]{:S(2)}, u32[]{:S(2)}) %all-to-all-start) | async-done | bytes 2359328 | tf_op jit(solution)/shard_map/all_to_all | solution.py:266
  288.5 1.4 copy-done.7
  289.9 47.6 %shard_map.245 = bf16[32,288,128]{2,1,0:T(8,128)(2,1)} custom-call(s32[1]{0:T(128)} %bitcast.1.par_ref, bf16[32,288,128]{2,1,0:T(8,128)(2,1)} %copy-done.7), custom_call_target="tpu_custom_call" | custom-call | flops 7247757312 | bytes 4718592 | tf_op jit(solution)/shard_map/pallas_call | solution.py:124
  337.5 4.4 all-to-all-start.1
  342.0 7.7 %fusion.105 = f32[192,1024]{1,0:T(8,128)} fusion(bf16[192,4096]{1,0:T(8,128)(2,1)} %copy-done.11, bf16[1024,4096]{1,0:T(8,128)(2,1)} %all-gather.8.cloned.1.call-done), kind=kOutput, calls=%fused_computation.160 | convolution fusion | flops 1610612736 | bytes 10747904 | tf_op jit(solution)/shard_map/dot_general | solution.py:190
  349.7 49.3 %all-to-all-done.1 = bf16[32,288,128]{2,1,0:T(8,128)(2,1)S(1)} async-done(((bf16[32,288,128]{2,1,0:T(8,128)(2,1)}), bf16[32,288,128]{2,1,0:T(8,128)(2,1)S(1)}, u32[]{:S(2)}, u32[]{:S(2)}) %all-to-all-start.1) | async-done | bytes 2359328 | tf_op jit(solution)/shard_map/all_to_all | solution.py:268
  399.9 2.2 copy.141
  402.1 1.4 convert_reduce_fusion
  403.5 1.8 copy.142
  405.4 2.2 slice_convert_fusion.3
  408.9 6.2 fusion.64
  416.2 2.1 convolution_convert_fusion.2
  418.3 3.8 fusion.1
  422.1 3.4 reshape.280
  425.5 2.2 copy.148
  427.7 4.2 all-to-all-start.4
  431.9 4.5 reshape_reshape.3
  436.4 3.8 copy.151
  440.2 30.1 %all-to-all-done.4 = bf16[32,16,2048]{2,1,0:T(8,128)(2,1)S(1)} async-done(((bf16[32,16,2048]{2,1,0:T(8,128)(2,1)}), bf16[32,16,2048]{2,1,0:T(8,128)(2,1)S(1)}, u32[]{:S(2)}, u32[]{:S(2)}) %all-to-all-start.4) | async-done | bytes 2097184 | tf_op jit(solution)/shard_map/all_to_all | solution.py:205
  470.3 1.3 copy-done.2
  471.6 4.4 all-to-all-start.6
  476.1 1.9 reduce_sum.177
  478.0 48.1 %all-to-all-done.6 = bf16[32,16,2048]{2,1,0:T(8,128)(2,1)S(1)} async-done(((bf16[32,16,2048]{2,1,0:T(8,128)(2,1)}), bf16[32,16,2048]{2,1,0:T(8,128)(2,1)S(1)}, u32[]{:S(2)}, u32[]{:S(2)}) %all-to-all-start.6) | async-done | bytes 2097184 | tf_op jit(solution)/shard_map/all_to_all | solution.py:205
  526.1 1.8 broadcast_in_dim.16
  528.1 4.8 all-to-all-start.5
  532.9 2.6 reshape.277
  535.6 1.6 copy.145
  537.2 26.3 %all-to-all-done.5 = bf16[32,16,2048]{2,1,0:T(8,128)(2,1)} async-done(((bf16[32,16,2048]{2,1,0:T(8,128)(2,1)}), bf16[32,16,2048]{2,1,0:T(8,128)(2,1)}, u32[]{:S(2)}, u32[]{:S(2)}) %all-to-all-start.5) | async-done | bytes 2097184 | tf_op jit(solution)/shard_map/all_to_all | solution.py:208
  563.4 4.1 all-to-all-start.2
  567.5 1.9 reduce_sum.178
  569.4 27.3 %all-to-all-done.2 = bf16[32,16,2176]{2,1,0:T(8,128)(2,1)S(1)} async-done(((bf16[32,16,2176]{2,1,0:T(8,128)(2,1)}), bf16[32,16,2176]{2,1,0:T(8,128)(2,1)S(1)}, u32[]{:S(2)}, u32[]{:S(2)}) %all-to-all-start.2) | async-done | bytes 2228256 | tf_op jit(solution)/shard_map/all_to_all | solution.py:205
  596.7 1.6 broadcast_in_dim.17
  598.3 4.8 all-to-all-start.7
  603.1 6.5 convolution_add_fusion.1
  610.0 22.7 %all-to-all-done.7 = bf16[32,16,2048]{2,1,0:T(8,128)(2,1)} async-done(((bf16[32,16,2048]{2,1,0:T(8,128)(2,1)}), bf16[32,16,2048]{2,1,0:T(8,128)(2,1)}, u32[]{:S(2)}, u32[]{:S(2)}) %all-to-all-start.7) | async-done | bytes 2097184 | tf_op jit(solution)/shard_map/all_to_all | solution.py:208
  632.7 1.5 broadcast_in_dim.15
  634.2 4.3 all-to-all-start.3
  638.5 2.6 fusion.90
  641.2 3.3 fusion.37
  644.5 2.1 convert_bitcast_fusion.2
  646.6 3.3 copy.149
  649.9 5.8 copy.163
  655.7 2.1 convert_bitcast_fusion.1
  657.8 5.5 copy.152
  663.3 6.4 reshape.286
  670.2 2.3 copy.146
  672.8 2.1 slice.224
  (155 shorter events, 19.8 us)
Async XLA Ops:
  7.2 1.6 copy-start.13
  7.2 1.6 copy-start.10
  7.2 67.3 %all-gather.8.cloned.1.call-start = ((), (), s32[]{:S(2)}) async-start(), calls=%async_computation.12 | async-start | bytes 10485760 | tf_op jit(solution)/shard_map/all_gather | solution.py:245
  7.9 130.0 %all-gather.10.cloned.1.call-start = ((), (), s32[]{:S(2)}) async-start(), calls=%async_computation.13 | async-start | bytes 10485760 | tf_op jit(solution)/shard_map/all_gather | solution.py:246
  8.7 1.7 copy-start.26
  8.7 2.0 copy-start.27
  8.7 2.2 copy-start.28
  8.7 2.4 copy-start.29
  8.7 2.6 copy-start.30
  8.7 2.8 copy-start.31
  8.7 3.0 copy-start.24
  8.8 3.2 copy-start.25
  8.8 11.1 %copy-start = (bf16[1,192,1024]{2,1,0:T(8,128)(2,1)S(1)}, bf16[1,192,1024]{2,1,0:T(8,128)(2,1)}, u32[]{:S(2)}) copy-start(bf16[1,192,1024]{2,1,0:T(8,128)(2,1)} %param.14) | copy-start | bytes 1179652
  8.8 193.2 %all-gather.6.cloned.1.call-start = ((), (), s32[]{:S(2)}) async-start(), calls=%async_computation.11 | async-start | bytes 10485760 | tf_op jit(solution)/shard_map/all_gather | solution.py:241
  10.4 411.7 %reduce-scatter.6.cloned.1.call-start = ((), (), s32[]{:S(2)}) async-start(), calls=%async_computation.15 | async-start | bytes 10485760 | tf_op jit(solution)/shard_map/reduce_scatter | solution.py:316
  20.2 185.2 %copy-start.18 = (f32[192]{0:T(256)}, f32[192]{0:T(256)S(1)}, u32[]{:S(2)}) copy-start(f32[192]{0:T(256)S(1)} %add_rsqrt_fusion) | copy-start | bytes 2308
  74.5 63.5 %copy-start.3 = (bf16[1,192,1024]{2,1,0:T(8,128)(2,1)S(1)}, bf16[1,192,1024]{2,1,0:T(8,128)(2,1)}, u32[]{:S(2)}) copy-start(bf16[1,192,1024]{2,1,0:T(8,128)(2,1)} %param.27) | copy-start | bytes 1179652
  87.2 68.9 %copy-start.6 = (bf16[192,4096]{1,0:T(8,128)(2,1)}, bf16[192,4096]{1,0:T(8,128)(2,1)S(1)}, u32[]{:S(2)}) copy-start(bf16[192,4096]{1,0:T(8,128)(2,1)S(1)} %get-tuple-element.33) | copy-start | bytes 4718596
  147.6 1.2 copy-start.11
  155.7 276.3 %reduce-scatter.8.cloned.1.call-start = ((), (), s32[]{:S(2)}) async-start(), calls=%async_computation.16 | async-start | bytes 10485760 | tf_op jit(solution)/shard_map/reduce_scatter | solution.py:316
  213.9 1.1 copy-start.14
  213.9 1.1 copy-start.17
  213.9 1.8 copy-start.9
  219.4 2.4 copy-start.5
  223.4 65.1 %all-to-all-start = ((bf16[32,288,128]{2,1,0:T(8,128)(2,1)}), bf16[32,288,128]{2,1,0:T(8,128)(2,1)S(1)}, u32[]{:S(2)}, u32[]{:S(2)}) async-start(bf16[32,288,128]{2,1,0:T(8,128)(2,1)} %pad_maximum_fusion), calls=%async_computation | async-start | bytes 4718592 | tf_op jit(solution)/shard_map/all_to_all | solution.py:266
  288.5 1.4 copy-start.7
  337.5 4.4 copy-start.4
  337.5 4.5 copy-start.22
  337.5 61.5 %all-to-all-start.1 = ((bf16[32,288,128]{2,1,0:T(8,128)(2,1)}), bf16[32,288,128]{2,1,0:T(8,128)(2,1)S(1)}, u32[]{:S(2)}, u32[]{:S(2)}) async-start(bf16[32,288,128]{2,1,0:T(8,128)(2,1)} %shard_map.245), calls=%async_computation.1 | async-start | bytes 4718592 | tf_op jit(solution)/shard_map/all_to_all | solution.py:268
  341.8 191.1 %reduce-scatter.4.cloned.1.call-start = ((), (), s32[]{:S(2)}) async-start(), calls=%async_computation.14 | async-start | bytes 11141120 | tf_op jit(solution)/shard_map/reduce_scatter | solution.py:316
  405.3 2.3 copy-start.15
  405.3 2.3 copy-start.16
  407.8 1.1 copy-start.12
  407.8 1.1 copy-start.19
  408.9 6.6 copy-start.8
  427.7 42.6 %all-to-all-start.4 = ((bf16[32,16,2048]{2,1,0:T(8,128)(2,1)}), bf16[32,16,2048]{2,1,0:T(8,128)(2,1)S(1)}, u32[]{:S(2)}, u32[]{:S(2)}) async-start(bf16[32,16,2048]{2,1,0:T(8,128)(2,1)} %bitcast.205), calls=%async_computation.6 | async-start | bytes 4194304 | tf_op jit(solution)/shard_map/all_to_all | solution.py:205
  470.3 1.3 copy-start.2
  471.6 54.5 %all-to-all-start.6 = ((bf16[32,16,2048]{2,1,0:T(8,128)(2,1)}), bf16[32,16,2048]{2,1,0:T(8,128)(2,1)S(1)}, u32[]{:S(2)}, u32[]{:S(2)}) async-start(bf16[32,16,2048]{2,1,0:T(8,128)(2,1)} %bitcast.206), calls=%async_computation.9 | async-start | bytes 4194304 | tf_op jit(solution)/shard_map/all_to_all | solution.py:205
  526.1 2.0 copy-start.1
  528.1 35.3 %all-to-all-start.5 = ((bf16[32,16,2048]{2,1,0:T(8,128)(2,1)}), bf16[32,16,2048]{2,1,0:T(8,128)(2,1)}, u32[]{:S(2)}, u32[]{:S(2)}) async-start(bf16[32,16,2048]{2,1,0:T(8,128)(2,1)} %broadcast_in_dim.16), calls=%async_computation.7 | async-start | bytes 4194304 | tf_op jit(solution)/shard_map/all_to_all | solution.py:208
  563.4 33.3 %all-to-all-start.2 = ((bf16[32,16,2176]{2,1,0:T(8,128)(2,1)}), bf16[32,16,2176]{2,1,0:T(8,128)(2,1)S(1)}, u32[]{:S(2)}, u32[]{:S(2)}) async-start(bf16[32,16,2176]{2,1,0:T(8,128)(2,1)} %bitcast.204), calls=%async_computation.3 | async-start | bytes 4456448 | tf_op jit(solution)/shard_map/all_to_all | solution.py:205
  569.4 33.6 %copy-start.21 = (f32[1,2,4,128]{3,2,1,0:T(4,128)S(1)}, f32[1,2,4,128]{3,2,1,0:T(4,128)}, u32[]{:S(2)}) copy-start(f32[1,2,4,128]{3,2,1,0:T(4,128)} %get-tuple-element.48) | copy-start | bytes 12292
  569.4 33.7 %copy-start.20 = (f32[1,2,4,128]{3,2,1,0:T(4,128)S(1)}, f32[1,2,4,128]{3,2,1,0:T(4,128)}, u32[]{:S(2)}) copy-start(f32[1,2,4,128]{3,2,1,0:T(4,128)} %get-tuple-element.47) | copy-start | bytes 12292
  598.3 34.4 %all-to-all-start.7 = ((bf16[32,16,2048]{2,1,0:T(8,128)(2,1)}), bf16[32,16,2048]{2,1,0:T(8,128)(2,1)}, u32[]{:S(2)}, u32[]{:S(2)}) async-start(bf16[32,16,2048]{2,1,0:T(8,128)(2,1)} %broadcast_in_dim.17), calls=%async_computation.10 | async-start | bytes 4194304 | tf_op jit(solution)/shard_map/all_to_all | solution.py:208
  634.2 35.5 %all-to-all-start.3 = ((bf16[32,16,2176]{2,1,0:T(8,128)(2,1)}), bf16[32,16,2176]{2,1,0:T(8,128)(2,1)S(1)}, u32[]{:S(2)}, u32[]{:S(2)}) async-start(bf16[32,16,2176]{2,1,0:T(8,128)(2,1)} %broadcast_in_dim.15), calls=%async_computation.4 | async-start | bytes 4456448 | tf_op jit(solution)/shard_map/all_to_all | solution.py:208
  675.8 3.3 copy-start.23
Sparse Core Ops, SparseCore 0:
  9.7 64.7 all-gather.7
  76.2 61.7 all-gather.9
  140.2 61.7 all-gather.5
  204.6 100.2 reduce-scatter.5
  307.6 103.7 reduce-scatter.7
  422.2 103.4 reduce-scatter.3
